TPU v7x, 32 devices: a whole 2x2x4 slice. The times are simulated.
32 devices in a mesh: grp: 2 (over x), cuts: 16 (over z, y, core).
Axes of the slice: x: 2, y: 2, z: 4, core: 2. Of those that a mesh axis runs over, the one named last changes fastest.
Arguments:
- stem_tensor: bfloat16 [2, 128, 32, 512], P(None, ('grp', 'cuts')), parts along dimension 1
- branch_tensors: bfloat16 [2, 2, 2, 512, 512], replicated, may hold values from -0.1875 to 0.1875
- cut_values: int32 [128, 2], P(('grp', 'cuts')), parts along dimension 0, may hold values from 0 to 1
- bit_rows: int32 [16384], P('grp'), parts along dimension 0, may hold values from 0 to 31
- bit_cols: int32 [16384], P('grp'), parts along dimension 0, may hold values from 0 to 511
Outputs:
- amplitudes: float32 [2, 16384], P(None, ('grp', 'cuts')), parts along dimension 1
- log_scale: float32 [2], P('grp'), parts along dimension 0
There are 2 independent parts, one for each index of `grp`. A program takes and returns all parts, laid end to end along the dimension named above; an argument that names none is the same for every part. Nothing has to cross between parts.
All inputs are finite; a program needn't handle non-finite values.
Results may differ from a plain program's by a relative error of at most 0.007.
Values sent between devices are 32-bit elements; how exact they have to be, the bound alone decides.
A program may use at most 128 MiB of HBM per device.

v0:
```python
import jax
import jax.numpy as jnp
from jax import lax
from jax.sharding import PartitionSpec as P


def joined(value, axis, join):
    pieces = lax.all_gather(value, axis)
    head = pieces[0]
    tail = pieces[1:]
    subtotal, _ = lax.scan(lambda subtotal, slab: (join(subtotal, slab), None), head, tail)
    return subtotal


def block_weights(matrices):
    blocks = []
    for value in range(2):
        real_w = matrices[value, 0]
        imag_w = matrices[value, 1]
        upper = jnp.concatenate([real_w, imag_w], axis=1)
        lower = jnp.concatenate([-imag_w, real_w], axis=1)
        blocks.append(jnp.concatenate([upper, lower], axis=0))
    return jnp.concatenate(blocks, axis=1)


def step_product(state, wide, values):
    slices, rows, double = state.shape
    flat = jnp.dot(state.reshape(slices * rows, double), wide, preferred_element_type=jnp.float32)
    flat = flat.reshape(slices, rows, 2 * double)
    picked = values[:, None, None] == 1
    return jnp.where(picked, flat[:, :, double:], flat[:, :, :double])


def add_tables(first, second):
    return first + second


def own_range(values):
    count = values.shape[0] // lax.axis_size("cuts")
    start = lax.axis_index("cuts") * count
    return lax.dynamic_slice_in_dim(values, start, count)


def shards(stem_tensor, branch_tensors, cut_values, bit_rows, bit_cols):
    width = stem_tensor.shape[3]
    state = jnp.concatenate([stem_tensor[0], stem_tensor[1]], axis=2)
    log_scale = jnp.zeros((1,), jnp.float32)
    total_steps = branch_tensors.shape[0]
    for step in range(total_steps):
        product = step_product(state, block_weights(branch_tensors[step]), cut_values[:, step])
        real_part = product[:, :, :width]
        imag_part = product[:, :, width:]
        local_peak = jnp.max(real_part * real_part + imag_part * imag_part)
        peak = jnp.sqrt(lax.pmax(local_peak, "cuts")) + 1e-06
        log_scale = log_scale + jnp.log(peak)
        if step + 1 < total_steps:
            state = (product / peak).astype(jnp.bfloat16)
    summed_slices = jnp.sum(product, axis=0)
    partial_value = jnp.stack([summed_slices[:, :width], summed_slices[:, width:]])
    flat = partial_value.reshape(2, partial_value.shape[1] * width)
    total = joined(flat, "cuts", add_tables)
    position = own_range(bit_rows) * width + own_range(bit_cols)
    amplitudes = total[:, position] / peak
    return (amplitudes, log_scale)


def solution(mesh):
    placed = (
        P(None, ("grp", "cuts"), None, None),
        P(),
        P(("grp", "cuts"), None),
        P("grp"),
        P("grp"),
    )
    return jax.shard_map(
        shards,
        mesh=mesh,
        in_specs=placed,
        out_specs=(P(None, ("grp", "cuts")), P("grp")),
        check_vma=False,
    )
```

profile of v0, /device:TPU:0, one launch (start us, length us, event | category | flops | bytes accessed | tf_op | source)
XLA Modules:
  0.0 112.8 jit_solution(15754800810012895437)
XLA Ops:
  7.2 0.0 all-gather.2.cloned.1.call-start
  7.2 2.7 %slice_bitcast_fusion.1 = (bf16[2,2,512,512]{3,2,1,0:T(8,128)(2,1)S(1)}, bf16[2,2,512,512]{3,2,1,0:T(8,128)(2,1)S(1)}) fusion(bf16[2,2,2,512,512]{4,3,2,1,0:T(8,128)(2,1)} %param.8), kind=kLoop, calls=%fused_computation.35 | loop fusion | bytes 8388608 | tf_op jit(solution)/shard_map/squeeze | solution.py:50
  9.9 0.0 copy-start.1
  9.9 0.0 copy-start
  9.9 0.1 fusion.40
  10.0 0.1 slice_bitcast_fusion.8
  10.1 0.4 copy-done.1
  10.6 0.3 copy-done
  10.9 0.7 fusion
  11.6 0.1 slice_select_fusion.1
  11.8 0.7 fusion.33
  12.4 1.0 slice_bitcast_fusion.4
  13.4 0.1 fusion.42
  13.5 35.6 %pmax.14 = f32[]{:T(128)} all-reduce(f32[]{:T(128)} %fusion.33), channel_id=1, replica_groups=mesh['grp'=2,'cuts'=16] {'cuts'}, use_global_device_ids=true, to_apply=%region_1.2 | all-reduce | flops 1 | bytes 8 | tf_op jit(solution)/shard_map/pmax | solution.py:54
  49.7 1.9 %fusion.15 = f32[4,32,2048]{2,1,0:T(8,128)S(1)} fusion(bf16[512,512]{1,0:T(8,128)(2,1)S(1)} %get-tuple-element.42, bf16[512,512]{1,0:T(8,128)(2,1)S(1)} %get-tuple-element.45, bf16[512,512]{1,0:T(8,128)(2,1)S(1)} %get-tuple-element.41, bf16[512,512]{1,0:T(8,128)(2,1)} %get-tuple-element.43, bf16[512,512]{1,0:T(8,128)(2,1)S(1)} %get-tuple-element.44, ...), kind=kOutput, calls=%fused_computation.19 | convolution fusion | flops 570687488 | bytes 4718596 | tf_op jit(solution)/shard_map/dot_general | solution.py:28
  51.6 0.1 fusion.44
  51.8 0.1 stack.9
  51.9 0.1 stack.10
  52.0 0.8 pad_maximum_fusion
  52.7 0.0 all-gather.2.cloned.1.call-update
  52.8 0.7 fusion.31
  53.4 30.5 %pmax.15 = f32[]{:T(128)} all-reduce(f32[]{:T(128)} %fusion.31), channel_id=1, replica_groups=mesh['grp'=2,'cuts'=16] {'cuts'}, use_global_device_ids=true, to_apply=%region_6.7 | all-reduce | flops 1 | bytes 8 | tf_op jit(solution)/shard_map/pmax | solution.py:54
  84.7 0.8 compare_select_fusion
  85.5 6.1 %all-gather.2.cloned.1.call-done = f32[16,2,16384]{2,1,0:T(2,128)} async-done(((f32[1,2,16384]{2,1,0:T(2,128)}), f32[16,2,16384]{2,1,0:T(2,128)}) %all-gather.2.cloned.1.call-update) | async-done | bytes 2097168 | tf_op jit(solution)/shard_map/all_gather | solution.py:8
  91.6 0.0 slice-start
  91.6 1.1 slice_bitcast_fusion.10
  92.6 0.5 slice-done
  93.2 1.5 %while.10 = (s32[]{:T(128)}, f32[2,16384]{1,0:T(2,128)S(1)}, f32[15,2,16384]{2,1,0:T(2,128)S(1)}, s32[]{:T(128)}) while((s32[]{:T(128)}, f32[2,16384]{1,0:T(2,128)S(1)}, f32[15,2,16384]{2,1,0:T(2,128)S(1)}, s32[]{:T(128)}) %tuple.42), condition=%wide.region_4.5_spmd, body=%wide.region_3.4_spmd.sunk | while | flops 32770 | bytes 393281 | solution.py:11
  93.2 0.1 bitcast_add_fusion.2
  93.3 0.1 bitcast_add_fusion.2
  93.4 0.1 bitcast_add_fusion.2
  93.5 0.1 bitcast_add_fusion.2
  93.6 0.1 bitcast_add_fusion.2
  93.7 0.1 bitcast_add_fusion.2
  93.8 0.1 bitcast_add_fusion.2
  93.9 0.1 bitcast_add_fusion.2
  94.0 0.1 bitcast_add_fusion.2
  94.1 0.1 bitcast_add_fusion.2
  94.2 0.1 bitcast_add_fusion.2
  94.3 0.1 bitcast_add_fusion.2
  94.4 0.1 bitcast_add_fusion.2
  94.5 0.1 bitcast_add_fusion.2
  94.6 0.1 bitcast_add_fusion.2
  94.7 5.0 %copy.9 = f32[2,16384]{0,1:T(8,128)} copy(f32[2,16384]{1,0:T(2,128)S(1)} %get-tuple-element.19) | data formatting | bytes 262144 | tf_op jit(solution)/shard_map/while | solution.py:11
  99.7 4.4 %gather_fusion = f32[512,2]{1,0:T(8,128)S(1)} fusion(f32[2,16384]{0,1:T(8,128)} %copy.9, s32[1024]{0:T(1024)S(1)} %pad_clamp_fusion), kind=kCustom, calls=%fused_computation | custom fusion | bytes 10240 | tf_op jit(solution)/shard_map/gather | solution.py:63
  104.1 0.7 copy.10
  (5 shorter events, 0.1 us)
Async XLA Ops:
  7.2 84.4 %all-gather.2.cloned.1.call-start = ((), (), s32[]{:S(2)}) async-start(), calls=%async_computation | async-start | bytes 2228224 | tf_op jit(solution)/shard_map/all_gather | solution.py:8
  9.9 0.7 copy-start.1
  9.9 1.0 copy-start
  91.6 1.6 %slice-start = ((f32[16,2,16384]{2,1,0:T(2,128)}), f32[15,2,16384]{2,1,0:T(2,128)S(1)}, s32[]{:S(2)}) async-start(f32[16,2,16384]{2,1,0:T(2,128)} %all-gather.2.cloned.1.call-done), calls=%async_computation.1 | async-start | bytes 3932160 | tf_op jit(solution)/shard_map/slice | solution.py:10
Sparse Core Ops, SparseCore 0:
  52.9 38.6 all-gather.1
where the time goes:
time: 113 us
  blocking collectives  66 us (58%)
  between operations  16.7 us (15%)
  local copies, waits for them, and re-layouts  16.3 us (14%)
  waiting for transfers between devices  6.12 us (5%)
  other arithmetic  4.58 us (4%)
  matrix products  2.64 us (2%)
    pmax x2, blocking collectives, shards(): peak = jnp.sqrt(lax.pmax(local_peak, 'cuts')) + 1e-06  66 us
    all_gather x1, waiting for transfers between devices, joined(): pieces = lax.all_gather(value, axis)  6.11 us
    while x1, local copies, waits for them, and re-layouts, joined(): lax.scan(lambda subtotal, slab: (join(subtotal, slab), None), head, tail)  4.95 us
    gather x1, local copies, waits for them, and re-layouts, shards(): amplitudes = total[:, position] / peak  4.41 us
    squeeze x1, local copies, waits for them, and re-layouts, shards(): branch_tensors[step]  2.68 us
    dot_general x2, matrix products, step_product(): jnp.dot(state.reshape(slices * rows, double), wide, preferred_element_typ...  2.64 us
  transfers between devices with their start and end apart: 1, of which 1 were waited for; matrix products, arithmetic and copies ran while one was open for 1% of the time, Pallas kernels for 0%

commit v1 on v0

v1 whole, which is shorter than its diff:
```python
import functools

import jax
import jax.numpy as jnp
from jax import lax
from jax.experimental import pallas as pl
from jax.experimental.pallas import tpu as pltpu
from jax.sharding import PartitionSpec as P

LANES = 128
LIFT = 2.0 ** 20


def complex_step(real_part, imag_part, weights):
    upper = jnp.concatenate([real_part, -imag_part], axis=1)
    lower = jnp.concatenate([imag_part, real_part], axis=1)
    left = jnp.concatenate([upper, lower], axis=0)
    return jnp.dot(left, weights, preferred_element_type=jnp.float32)


def largest(values):
    return jnp.max(jnp.max(values, axis=0, keepdims=True), axis=1, keepdims=True)


def kernel(n, group, cut_hbm, stem_hbm, branch_hbm, rows_hbm, cols_hbm, amp_ref, log_ref,
           cut_s, stem_v, early_v, later_v, rows_v, cols_v, outgoing, incoming, load_sems, send_sems, recv_sems):
    me = lax.axis_index("cuts")
    slices, rows, width = stem_hbm.shape[1], stem_hbm.shape[2], stem_hbm.shape[3]
    mine = amp_ref.shape[1]
    lines = mine // LANES

    stem_load = pltpu.make_async_copy(stem_hbm, stem_v, load_sems.at[0])
    cut_load = pltpu.make_async_copy(cut_hbm, cut_s, load_sems.at[1])
    rows_load = pltpu.make_async_copy(rows_hbm, rows_v, load_sems.at[2])
    cols_load = pltpu.make_async_copy(cols_hbm, cols_v, load_sems.at[3])
    branch_loads = [
        pltpu.make_async_copy(branch_hbm.at[step], held, load_sems.at[4 + step])
        for step, held in enumerate((early_v, later_v))
    ]
    cut_load.start()
    stem_load.start()
    branch_loads[0].start()
    cols_load.start()
    rows_load.start()
    branch_loads[1].start()

    barrier = pltpu.get_barrier_semaphore()

    def greet(k, carry):
        pl.semaphore_signal(barrier, inc=1, device_id={"cuts": lax.rem(me + k, n)}, device_id_type=pl.DeviceIdType.MESH)
        return carry

    lax.fori_loop(1, n, greet, 0)

    cut_load.wait()
    stem_load.wait()
    branch_loads[0].wait()
    first = []
    for s in range(slices):
        weights = early_v[cut_s[0, s]].reshape(2 * width, width)
        first.append(complex_step(stem_v[0, s], stem_v[1, s], weights))
    branch_loads[1].wait()
    second = []
    for s in range(slices):
        state = (first[s] * LIFT).astype(jnp.bfloat16)
        weights = later_v[cut_s[1, s]].reshape(2 * width, width)
        second.append(complex_step(state[:rows], state[rows:], weights))

    square = functools.reduce(jnp.maximum, [p[:rows] * p[:rows] + p[rows:] * p[rows:] for p in first])
    peak_square = largest(square)
    own_peak = jnp.sqrt(peak_square) + 1e-06
    shrink = (1.0 / LIFT) / own_peak
    shrunk = [p * shrink for p in second]
    square = functools.reduce(jnp.maximum, [p[:rows] * p[:rows] + p[rows:] * p[rows:] for p in shrunk])
    raw_second = jnp.sqrt(largest(square)) * own_peak
    stats = jnp.concatenate(
        [jnp.broadcast_to(peak_square, (1, LANES)), jnp.broadcast_to(raw_second, (1, LANES))], axis=0)

    table = functools.reduce(jnp.add, second)
    high = table.astype(jnp.bfloat16)
    low = (table - high.astype(jnp.float32)).astype(jnp.bfloat16)
    left = jnp.concatenate([high, low], axis=0)

    cols_load.wait()
    rows_load.wait()
    pl.semaphore_wait(barrier, n - 1)

    def picked(dest):
        col_lines = cols_v[dest]
        row_lines = rows_v[dest]
        column = lax.broadcasted_iota(jnp.int32, (width, LANES), 0)
        row = lax.broadcasted_iota(jnp.int32, (rows, LANES), 0)
        hot = jnp.concatenate(
            [jnp.where(column == col_lines[j:j + 1], 1.0, 0.0).astype(jnp.bfloat16) for j in range(lines)], axis=1)
        found = jnp.dot(left, hot, preferred_element_type=jnp.float32)
        found = found[:2 * rows] + found[2 * rows:]
        chosen = jnp.concatenate([row == row_lines[j:j + 1] for j in range(lines)], axis=1)
        parts = [jnp.sum(jnp.where(chosen, found[p * rows:(p + 1) * rows], 0.0), axis=0, keepdims=True) for p in range(2)]
        return jnp.concatenate(parts, axis=0)

    def remote(dest):
        return pltpu.make_async_remote_copy(
            src_ref=outgoing.at[dest],
            dst_ref=incoming.at[me],
            send_sem=send_sems.at[dest],
            recv_sem=recv_sems.at[me],
            device_id={"cuts": dest},
            device_id_type=pl.DeviceIdType.MESH,
        )

    def serve(start, count):
        dests = [lax.rem(me + start + i, n) for i in range(count)]
        for dest in dests:
            outgoing[dest, :, :mine] = picked(dest)
            outgoing[dest, :, mine:] = stats
        for dest in dests:
            remote(dest).start()

    def serve_group(g, carry):
        serve(1 + g * group, group)
        return carry

    rounds = (n - 1) // group
    lax.fori_loop(0, rounds, serve_group, 0)
    serve(1 + rounds * group, n - 1 - rounds * group)
    incoming[me, :, :mine] = picked(me)
    incoming[me, :, mine:] = stats

    def receive(k, carry):
        source = lax.rem(me + k, n)
        pltpu.make_async_remote_copy(
            src_ref=outgoing.at[source],
            dst_ref=incoming.at[source],
            send_sem=send_sems.at[source],
            recv_sem=recv_sems.at[source],
            device_id={"cuts": source},
            device_id_type=pl.DeviceIdType.MESH,
        ).wait()
        return carry

    lax.fori_loop(1, n, receive, 0)
    total = jnp.sum(incoming[:, :, :mine], axis=0)
    peaks = jnp.max(incoming[:, :, mine:], axis=0)
    first_peak = jnp.sqrt(peaks[0:1, 0:1]) + 1e-06
    second_peak = peaks[1:2, 0:1] / first_peak + 1e-06
    amp_ref[...] = total * ((1.0 / LIFT) / first_peak) / second_peak
    log_ref[...] = jnp.log(first_peak) + jnp.log(second_peak)


def shards(stem_tensor, branch_tensors, cut_values, bit_rows, bit_cols):
    n = lax.axis_size("cuts")
    slices = stem_tensor.shape[1]
    mine = bit_rows.shape[0] // n
    steps = branch_tensors.shape[0]
    any_spec = pl.BlockSpec(memory_space=pl.ANY)
    lined = (n, mine // LANES, LANES)
    amplitudes, log_scale = pl.pallas_call(
        functools.partial(kernel, n, 5),
        out_shape=(
            jax.ShapeDtypeStruct((2, mine), jnp.float32),
            jax.ShapeDtypeStruct((1, 1), jnp.float32),
        ),
        in_specs=[any_spec] * 5,
        out_specs=(pl.BlockSpec(memory_space=pltpu.VMEM), pl.BlockSpec(memory_space=pltpu.VMEM)),
        scratch_shapes=[
            pltpu.SMEM((steps, slices), jnp.int32),
            pltpu.VMEM(stem_tensor.shape, jnp.bfloat16),
            pltpu.VMEM(branch_tensors.shape[1:], jnp.bfloat16),
            pltpu.VMEM(branch_tensors.shape[1:], jnp.bfloat16),
            pltpu.VMEM(lined, jnp.int32),
            pltpu.VMEM(lined, jnp.int32),
            pltpu.VMEM((n, 2, mine + LANES), jnp.float32),
            pltpu.VMEM((n, 2, mine + LANES), jnp.float32),
            pltpu.SemaphoreType.DMA((4 + steps,)),
            pltpu.SemaphoreType.DMA((n,)),
            pltpu.SemaphoreType.DMA((n,)),
        ],
        compiler_params=pltpu.CompilerParams(
            collective_id=0, has_side_effects=True, vmem_limit_bytes=56 * 1024 * 1024
        ),
    )(cut_values.T, stem_tensor, branch_tensors, bit_rows.reshape(lined), bit_cols.reshape(lined))
    return (amplitudes, log_scale.reshape(1))


def solution(mesh):
    placed = (
        P(None, ("grp", "cuts"), None, None),
        P(),
        P(("grp", "cuts"), None),
        P("grp"),
        P("grp"),
    )
    return jax.shard_map(
        shards,
        mesh=mesh,
        in_specs=placed,
        out_specs=(P(None, ("grp", "cuts")), P("grp")),
        check_vma=False,
    )
```

time: 113 us -> 16.7 us (0.15)
  blocking collectives: 66 us -> 0 us
  local copies, waits for them, and re-layouts: 16.3 us -> 1.26 us
  between operations: 16.7 us -> 2.4 us
  Pallas kernels: 0 us -> 12.9 us
  waiting for transfers between devices: 6.12 us -> 0 us
  other arithmetic: 4.58 us -> 0 us
  matrix products: 2.64 us -> 0 us
    pmax x2 -> x0, blocking collectives: 66 us -> none  [shards(): peak = jnp.sqrt(lax.pmax(local_peak, 'cuts')) + 1e-06]
    pallas_call x0 -> x1, Pallas kernels: none -> 12.9 us  [shards(): pl.pallas_call(functools.partial(kernel, n, 5), out_shape=(jax.ShapeDtype...]
    all_gather x1 -> x0, waiting for transfers between devices: 6.11 us -> none  [joined(): pieces = lax.all_gather(value, axis)]
    while x1 -> x0, local copies, waits for them, and re-layouts: 4.95 us -> none  [joined(): lax.scan(lambda subtotal, slab: (join(subtotal, slab), None), head, tail)]
    squeeze x4 -> x0, local copies, waits for them, and re-layouts: 4.83 us -> none  [the longest x1 2.68 us: shards(): branch_tensors[step]]
    gather x1 -> x0, local copies, waits for them, and re-layouts: 4.41 us -> none  [shards(): amplitudes = total[:, position] / peak]
    dot_general x2 -> x0, matrix products: 2.64 us -> none  [step_product(): jnp.dot(state.reshape(slices * rows, double), wide, preferred_element_typ...]
    reduce_max x2 -> x0, other arithmetic: 1.34 us -> none  [shards(): local_peak = jnp.max(real_part * real_part + imag_part * imag_part)]
  transfers between devices with their start and end apart: 1 -> 0, of which waited for: 1 -> 0; matrix products, arithmetic and copies ran while one was open for 1% -> 0% of each run, Pallas kernels for 0% -> 0%
where the time goes in v1:
time: 16.7 us; the launch traced here: 16.5 us
  Pallas kernels  12.9 us (77%)
  between operations  2.4 us (14%)
  local copies, waits for them, and re-layouts  1.26 us (8%)
    pallas_call x1, Pallas kernels, shards(): pl.pallas_call(functools.partial(kernel, n, 5), out_shape=(jax.ShapeDtype...  12.9 us
    unnamed x1, local copies, waits for them, and re-layouts  1.26 us

profile of v1, /device:TPU:0, one launch (start us, length us, event | category | flops | bytes accessed | tf_op | source)
XLA Modules:
  0.0 16.5 jit_solution(7254112125078299012)
XLA Ops:
  0.6 12.9 %shard_map.68 = (f32[2,512]{1,0:T(2,128)}, f32[1,1]{1,0:T(1,128)}) custom-call(s32[2,4]{1,0:T(2,128)} %bitcast.6, bf16[2,4,32,512]{3,2,1,0:T(8,128)(2,1)} %stem_hbm.1, bf16[2,2,2,512,512]{4,3,2,1,0:T(8,128)(2,1)} %branch_hbm.1, s32[16,4,128]{2,1,0:T(4,128)} %bitcast.4, s32[16,4,128]{2,1,0:T(4,128)} %bitcast.5), custom_call_target="tpu_custom_call" | custom-call | tf_op jit(solution)/shard_map/pallas_call | solution.py:157
  13.5 1.3 %copy.9 = f32[2,512]{1,0:T(2,128)} copy(f32[2,512]{1,0:T(2,128)} %get-tuple-element.8) | data formatting | bytes 8192

commit v2 on v1

--- a/solution.py
+++ b/solution.py
@@ -22,11 +22,11 @@
     return jnp.max(jnp.max(values, axis=0, keepdims=True), axis=1, keepdims=True)
 
 
-def kernel(n, group, cut_hbm, stem_hbm, branch_hbm, rows_hbm, cols_hbm, amp_ref, log_ref,
+def kernel(n, group, cut_hbm, stem_hbm, branch_hbm, rows_hbm, cols_hbm, out_ref,
            cut_s, stem_v, early_v, later_v, rows_v, cols_v, outgoing, incoming, load_sems, send_sems, recv_sems):
     me = lax.axis_index("cuts")
     slices, rows, width = stem_hbm.shape[1], stem_hbm.shape[2], stem_hbm.shape[3]
-    mine = amp_ref.shape[1]
+    mine = out_ref.shape[1] - LANES
     lines = mine // LANES
 
     stem_load = pltpu.make_async_copy(stem_hbm, stem_v, load_sems.at[0])
@@ -139,12 +139,23 @@
         return carry
 
     lax.fori_loop(1, n, receive, 0)
-    total = jnp.sum(incoming[:, :, :mine], axis=0)
-    peaks = jnp.max(incoming[:, :, mine:], axis=0)
+    out_ref[:, :mine] = jnp.sum(incoming[:, :, :mine], axis=0)
+    out_ref[:, mine:] = jnp.max(incoming[:, :, mine:], axis=0)
+
+
+def finish(sum_ref, amp_hbm, log_hbm, amp_v, log_v, sems):
+    mine = amp_v.shape[1]
+    peaks = sum_ref[:, mine:]
     first_peak = jnp.sqrt(peaks[0:1, 0:1]) + 1e-06
     second_peak = peaks[1:2, 0:1] / first_peak + 1e-06
-    amp_ref[...] = total * ((1.0 / LIFT) / first_peak) / second_peak
-    log_ref[...] = jnp.log(first_peak) + jnp.log(second_peak)
+    log_v[...] = jnp.log(first_peak) + jnp.log(second_peak)
+    log_store = pltpu.make_async_copy(log_v, log_hbm, sems.at[0])
+    log_store.start()
+    amp_v[...] = sum_ref[:, :mine] * ((1.0 / LIFT) / first_peak) / second_peak
+    amp_store = pltpu.make_async_copy(amp_v, amp_hbm, sems.at[1])
+    amp_store.start()
+    log_store.wait()
+    amp_store.wait()
 
 
 def shards(stem_tensor, branch_tensors, cut_values, bit_rows, bit_cols):
@@ -154,14 +165,11 @@
     steps = branch_tensors.shape[0]
     any_spec = pl.BlockSpec(memory_space=pl.ANY)
     lined = (n, mine // LANES, LANES)
-    amplitudes, log_scale = pl.pallas_call(
+    sums = pl.pallas_call(
         functools.partial(kernel, n, 5),
-        out_shape=(
-            jax.ShapeDtypeStruct((2, mine), jnp.float32),
-            jax.ShapeDtypeStruct((1, 1), jnp.float32),
-        ),
+        out_shape=pltpu.VMEM((2, mine + LANES), jnp.float32),
         in_specs=[any_spec] * 5,
-        out_specs=(pl.BlockSpec(memory_space=pltpu.VMEM), pl.BlockSpec(memory_space=pltpu.VMEM)),
+        out_specs=pl.BlockSpec(memory_space=pltpu.VMEM),
         scratch_shapes=[
             pltpu.SMEM((steps, slices), jnp.int32),
             pltpu.VMEM(stem_tensor.shape, jnp.bfloat16),
@@ -179,6 +187,20 @@
             collective_id=0, has_side_effects=True, vmem_limit_bytes=56 * 1024 * 1024
         ),
     )(cut_values.T, stem_tensor, branch_tensors, bit_rows.reshape(lined), bit_cols.reshape(lined))
+    amplitudes, log_scale = pl.pallas_call(
+        finish,
+        out_shape=(
+            jax.ShapeDtypeStruct((2, mine), jnp.float32),
+            jax.ShapeDtypeStruct((1, 1), jnp.float32),
+        ),
+        in_specs=[pl.BlockSpec(memory_space=pltpu.VMEM)],
+        out_specs=(any_spec, any_spec),
+        scratch_shapes=[
+            pltpu.VMEM((2, mine), jnp.float32),
+            pltpu.VMEM((1, 1), jnp.float32),
+            pltpu.SemaphoreType.DMA((2,)),
+        ],
+    )(sums)
     return (amplitudes, log_scale.reshape(1))
 
 

time: 16.7 us -> 15 us (0.90)
  between operations: 2.4 us -> 0.65 us
  Pallas kernels: 12.9 us -> 13.6 us
  local copies, waits for them, and re-layouts: 1.26 us -> 0.58 us
    pallas_call x1 -> x2, Pallas kernels: 12.9 us -> 13.6 us  [the longest x1 12.2 us: shards(): pl.pallas_call(functools.partial(kernel, n, 5), out_shape=pltpu.VMEM((2,...]
    unnamed x1 -> x2, local copies, waits for them, and re-layouts: 1.26 us -> 0.58 us
where the time goes in v2:
time: 15 us; the launch traced here: 14.8 us
  Pallas kernels  13.6 us (91%)
  between operations  0.65 us (4%)
  local copies, waits for them, and re-layouts  0.58 us (4%)
    pallas_call x1, Pallas kernels, shards(): pl.pallas_call(functools.partial(kernel, n, 5), out_shape=pltpu.VMEM((2,...  12.2 us
    pallas_call x1, Pallas kernels, shards(): pl.pallas_call(finish, out_shape=(jax.ShapeDtypeStruct((2, mine), jnp.flo...  1.36 us
    unnamed x2, local copies, waits for them, and re-layouts  0.58 us

profile of v2, /device:TPU:0, one launch (start us, length us, event | category | flops | bytes accessed | tf_op | source)
XLA Modules:
  0.0 14.8 jit_solution(14873228692392271014)
XLA Ops:
  0.6 12.2 %shard_map.68.sum_ref = f32[2,640]{1,0:T(2,128)S(1)} custom-call(s32[2,4]{1,0:T(2,128)} %bitcast.6, bf16[2,4,32,512]{3,2,1,0:T(8,128)(2,1)} %stem_hbm.1, bf16[2,2,2,512,512]{4,3,2,1,0:T(8,128)(2,1)} %branch_hbm.1, s32[16,4,128]{2,1,0:T(4,128)} %bitcast.4, s32[16,4,128]{2,1,0:T(4,128)} %bitcast.5), custom_call_target="tpu_custom_call" | custom-call | tf_op jit(solution)/shard_map/pallas_call | solution.py:168
  12.9 0.0 copy-start
  12.9 0.6 %copy-done = f32[2,640]{1,0:T(2,128)} copy-done((f32[2,640]{1,0:T(2,128)}, f32[2,640]{1,0:T(2,128)S(1)}, u32[]{:S(2)}) %copy-start) | copy-done | bytes 5144
  13.5 1.4 %shard_map.69 = (f32[2,512]{1,0:T(2,128)}, f32[1,1]{1,0:T(1,128)}) custom-call(f32[2,640]{1,0:T(2,128)} %copy-done), custom_call_target="tpu_custom_call" | custom-call | tf_op jit(solution)/shard_map/pallas_call | solution.py:190
Async XLA Ops:
  12.9 0.6 %copy-start = (f32[2,640]{1,0:T(2,128)}, f32[2,640]{1,0:T(2,128)S(1)}, u32[]{:S(2)}) copy-start(f32[2,640]{1,0:T(2,128)S(1)} %shard_map.68.sum_ref) | copy-start | bytes 15364

commit v3 on v2

--- a/solution.py
+++ b/solution.py
@@ -23,26 +23,26 @@
 
 
 def kernel(n, group, cut_hbm, stem_hbm, branch_hbm, rows_hbm, cols_hbm, out_ref,
-           cut_s, stem_v, early_v, later_v, rows_v, cols_v, outgoing, incoming, load_sems, send_sems, recv_sems):
+           cut_s, stem_v, early_v, later_v, rows_v, cols_v, hot_v, outgoing, incoming, load_sems, send_sems, recv_sems):
     me = lax.axis_index("cuts")
     slices, rows, width = stem_hbm.shape[1], stem_hbm.shape[2], stem_hbm.shape[3]
     mine = out_ref.shape[1] - LANES
     lines = mine // LANES
 
-    stem_load = pltpu.make_async_copy(stem_hbm, stem_v, load_sems.at[0])
-    cut_load = pltpu.make_async_copy(cut_hbm, cut_s, load_sems.at[1])
-    rows_load = pltpu.make_async_copy(rows_hbm, rows_v, load_sems.at[2])
-    cols_load = pltpu.make_async_copy(cols_hbm, cols_v, load_sems.at[3])
+    cols_load = pltpu.make_async_copy(cols_hbm, cols_v, load_sems.at[0])
+    rows_load = pltpu.make_async_copy(rows_hbm, rows_v, load_sems.at[1])
+    cut_load = pltpu.make_async_copy(cut_hbm, cut_s, load_sems.at[2])
+    stem_load = pltpu.make_async_copy(stem_hbm, stem_v, load_sems.at[3])
     branch_loads = [
-        pltpu.make_async_copy(branch_hbm.at[step], held, load_sems.at[4 + step])
+        [
+            pltpu.make_async_copy(
+                branch_hbm.at[step, value, part], held.at[value, part], load_sems.at[4 + 4 * step + 2 * value + part])
+            for value in range(2) for part in range(2)
+        ]
         for step, held in enumerate((early_v, later_v))
     ]
-    cut_load.start()
-    stem_load.start()
-    branch_loads[0].start()
-    cols_load.start()
-    rows_load.start()
-    branch_loads[1].start()
+    for load in [cols_load, stem_load, cut_load] + branch_loads[0] + [rows_load] + branch_loads[1]:
+        load.start()
 
     barrier = pltpu.get_barrier_semaphore()
 
@@ -52,14 +52,31 @@
 
     lax.fori_loop(1, n, greet, 0)
 
+    def hot_columns(dest):
+        col_lines = cols_v[dest]
+        column = lax.broadcasted_iota(jnp.int16, (width, LANES), 0)
+        one, zero = jnp.bfloat16(1), jnp.bfloat16(0)
+        lanes = [jnp.broadcast_to(col_lines[j:j + 1], (width, LANES)).astype(jnp.int16) for j in range(lines)]
+        return jnp.concatenate([jnp.where(column == line, one, zero) for line in lanes], axis=1)
+
+    def keep_hot(k, carry):
+        hot_v[k] = hot_columns(lax.rem(me + 1 + k, n))
+        return carry
+
+    cols_load.wait()
+    if hot_v.shape[0] == n:
+        lax.fori_loop(0, n, keep_hot, 0)
+
     cut_load.wait()
     stem_load.wait()
-    branch_loads[0].wait()
+    for load in branch_loads[0]:
+        load.wait()
     first = []
     for s in range(slices):
         weights = early_v[cut_s[0, s]].reshape(2 * width, width)
         first.append(complex_step(stem_v[0, s], stem_v[1, s], weights))
-    branch_loads[1].wait()
+    for load in branch_loads[1]:
+        load.wait()
     second = []
     for s in range(slices):
         state = (first[s] * LIFT).astype(jnp.bfloat16)
@@ -81,17 +98,12 @@
     low = (table - high.astype(jnp.float32)).astype(jnp.bfloat16)
     left = jnp.concatenate([high, low], axis=0)
 
-    cols_load.wait()
     rows_load.wait()
     pl.semaphore_wait(barrier, n - 1)
 
-    def picked(dest):
-        col_lines = cols_v[dest]
+    def picked(dest, hot):
         row_lines = rows_v[dest]
-        column = lax.broadcasted_iota(jnp.int32, (width, LANES), 0)
         row = lax.broadcasted_iota(jnp.int32, (rows, LANES), 0)
-        hot = jnp.concatenate(
-            [jnp.where(column == col_lines[j:j + 1], 1.0, 0.0).astype(jnp.bfloat16) for j in range(lines)], axis=1)
         found = jnp.dot(left, hot, preferred_element_type=jnp.float32)
         found = found[:2 * rows] + found[2 * rows:]
         chosen = jnp.concatenate([row == row_lines[j:j + 1] for j in range(lines)], axis=1)
@@ -109,21 +121,26 @@
         )
 
     def serve(start, count):
-        dests = [lax.rem(me + start + i, n) for i in range(count)]
-        for dest in dests:
-            outgoing[dest, :, :mine] = picked(dest)
+        dests = [lax.rem(me + 1 + start + i, n) for i in range(count)]
+        for i, dest in enumerate(dests):
+            hot = hot_v[start + i] if hot_v.shape[0] == n else hot_columns(dest)
+            outgoing[dest, :, :mine] = picked(dest, hot)
             outgoing[dest, :, mine:] = stats
         for dest in dests:
             remote(dest).start()
 
     def serve_group(g, carry):
-        serve(1 + g * group, group)
+        serve(g * group, group)
         return carry
 
     rounds = (n - 1) // group
-    lax.fori_loop(0, rounds, serve_group, 0)
-    serve(1 + rounds * group, n - 1 - rounds * group)
-    incoming[me, :, :mine] = picked(me)
+    if hot_v.shape[0] == n:
+        for g in range(rounds):
+            serve(g * group, group)
+    else:
+        lax.fori_loop(0, rounds, serve_group, 0)
+    serve(rounds * group, n - 1 - rounds * group)
+    incoming[me, :, :mine] = picked(me, hot_v[n - 1] if hot_v.shape[0] == n else hot_columns(me))
     incoming[me, :, mine:] = stats
 
     def receive(k, carry):
@@ -163,10 +180,11 @@
     slices = stem_tensor.shape[1]
     mine = bit_rows.shape[0] // n
     steps = branch_tensors.shape[0]
+    width = stem_tensor.shape[3]
     any_spec = pl.BlockSpec(memory_space=pl.ANY)
     lined = (n, mine // LANES, LANES)
     sums = pl.pallas_call(
-        functools.partial(kernel, n, 5),
+        functools.partial(kernel, n, 3),
         out_shape=pltpu.VMEM((2, mine + LANES), jnp.float32),
         in_specs=[any_spec] * 5,
         out_specs=pl.BlockSpec(memory_space=pltpu.VMEM),
@@ -177,9 +195,10 @@
             pltpu.VMEM(branch_tensors.shape[1:], jnp.bfloat16),
             pltpu.VMEM(lined, jnp.int32),
             pltpu.VMEM(lined, jnp.int32),
+            pltpu.VMEM((n if n <= 16 else 1, width, mine), jnp.bfloat16),
             pltpu.VMEM((n, 2, mine + LANES), jnp.float32),
             pltpu.VMEM((n, 2, mine + LANES), jnp.float32),
-            pltpu.SemaphoreType.DMA((4 + steps,)),
+            pltpu.SemaphoreType.DMA((4 + 4 * steps,)),
             pltpu.SemaphoreType.DMA((n,)),
             pltpu.SemaphoreType.DMA((n,)),
         ],
@@ -200,7 +219,7 @@
             pltpu.VMEM((1, 1), jnp.float32),
             pltpu.SemaphoreType.DMA((2,)),
         ],
-    )(sums)
+    )(pltpu.with_memory_space_constraint(sums, pltpu.VMEM))
     return (amplitudes, log_scale.reshape(1))
 
 

time: 15 us -> 13.5 us (0.900)
  Pallas kernels: 13.6 us -> 12.7 us
  local copies, waits for them, and re-layouts: 0.58 us -> 0 us
    pallas_call x1, Pallas kernels: 1.36 us -> 0.67 us  [shards(): pl.pallas_call(finish, out_shape=(jax.ShapeDtypeStruct((2, mine), jnp.flo...]
    unnamed x2 -> x0, local copies, waits for them, and re-layouts: 0.58 us -> none
    pallas_call x1, Pallas kernels: 12.2 us -> 12.1 us  [shards(): pl.pallas_call(functools.partial(kernel, n, 3), out_shape=pltpu.VMEM((2,...]
where the time goes in v3:
time: 13.5 us; the launch traced here: 13.4 us
  Pallas kernels  12.7 us (94%)
  between operations  0.64 us (5%)
    pallas_call x1, Pallas kernels, shards(): pl.pallas_call(functools.partial(kernel, n, 3), out_shape=pltpu.VMEM((2,...  12.1 us
    pallas_call x1, Pallas kernels, shards(): pl.pallas_call(finish, out_shape=(jax.ShapeDtypeStruct((2, mine), jnp.flo...  0.67 us

profile of v3, /device:TPU:0, one launch (start us, length us, event | category | flops | bytes accessed | tf_op | source)
XLA Modules:
  0.0 13.4 jit_solution(14276142170032243627)
XLA Ops:
  0.6 12.1 %shard_map.68.sum_ref = f32[2,640]{1,0:T(2,128)S(1)} custom-call(s32[2,4]{1,0:T(2,128)} %bitcast.6, bf16[2,4,32,512]{3,2,1,0:T(8,128)(2,1)} %stem_hbm.1, bf16[2,2,2,512,512]{4,3,2,1,0:T(8,128)(2,1)} %branch_hbm.1, s32[16,4,128]{2,1,0:T(4,128)} %bitcast.4, s32[16,4,128]{2,1,0:T(4,128)} %bitcast.5), custom_call_target="tpu_custom_call" | custom-call | tf_op jit(solution)/shard_map/pallas_call | solution.py:186
  12.7 0.7 %shard_map.69 = (f32[2,512]{1,0:T(2,128)}, f32[1,1]{1,0:T(1,128)}) custom-call(f32[2,640]{1,0:T(2,128)S(1)} %shard_map.68.sum_ref), custom_call_target="tpu_custom_call" | custom-call | tf_op jit(solution)/shard_map/pallas_call | solution.py:209

commit v4 on v3

--- a/solution.py
+++ b/solution.py
@@ -23,7 +23,7 @@
 
 
 def kernel(n, group, cut_hbm, stem_hbm, branch_hbm, rows_hbm, cols_hbm, out_ref,
-           cut_s, stem_v, early_v, later_v, rows_v, cols_v, hot_v, outgoing, incoming, load_sems, send_sems, recv_sems):
+           cut_s, stem_v, early_v, later_v, rows_v, cols_v, hot_v, outgoing, incoming, load_sems, send_sem, recv_sem):
     me = lax.axis_index("cuts")
     slices, rows, width = stem_hbm.shape[1], stem_hbm.shape[2], stem_hbm.shape[3]
     mine = out_ref.shape[1] - LANES
@@ -54,13 +54,18 @@
 
     def hot_columns(dest):
         col_lines = cols_v[dest]
-        column = lax.broadcasted_iota(jnp.int16, (width, LANES), 0)
+        column = lax.broadcasted_iota(jnp.int16, (LANES, LANES), 0)
         one, zero = jnp.bfloat16(1), jnp.bfloat16(0)
-        lanes = [jnp.broadcast_to(col_lines[j:j + 1], (width, LANES)).astype(jnp.int16) for j in range(lines)]
+        low_part = lax.rem(col_lines, LANES)
+        lanes = [jnp.broadcast_to(low_part[j:j + 1], (LANES, LANES)).astype(jnp.int16) for j in range(lines)]
         return jnp.concatenate([jnp.where(column == line, one, zero) for line in lanes], axis=1)
 
-    def keep_hot(k, carry):
-        hot_v[k] = hot_columns(lax.rem(me + 1 + k, n))
+    def nth_dest(i):
+        swing = (i + 1) // 2
+        return lax.rem(me + n // 2 + swing * (1 - 2 * (i % 2)) + n, n)
+
+    def keep_hot(i, carry):
+        hot_v[i] = hot_columns(nth_dest(i))
         return carry
 
     cols_load.wait()
@@ -96,32 +101,38 @@
     table = functools.reduce(jnp.add, second)
     high = table.astype(jnp.bfloat16)
     low = (table - high.astype(jnp.float32)).astype(jnp.bfloat16)
-    left = jnp.concatenate([high, low], axis=0)
+    blocks = width // LANES
+
+    def blocked(half):
+        return jnp.concatenate(
+            [half[p * rows:(p + 1) * rows, c * LANES:(c + 1) * LANES] for p in range(2) for c in range(blocks)], axis=0)
+
+    left = jnp.concatenate([blocked(high), blocked(low)], axis=1)
 
     rows_load.wait()
     pl.semaphore_wait(barrier, n - 1)
 
     def picked(dest, hot):
-        row_lines = rows_v[dest]
-        row = lax.broadcasted_iota(jnp.int32, (rows, LANES), 0)
-        found = jnp.dot(left, hot, preferred_element_type=jnp.float32)
-        found = found[:2 * rows] + found[2 * rows:]
-        chosen = jnp.concatenate([row == row_lines[j:j + 1] for j in range(lines)], axis=1)
-        parts = [jnp.sum(jnp.where(chosen, found[p * rows:(p + 1) * rows], 0.0), axis=0, keepdims=True) for p in range(2)]
+        spots = blocks * rows
+        spot_lines = (cols_v[dest] // LANES) * rows + rows_v[dest]
+        spot = lax.broadcasted_iota(jnp.int32, (spots, LANES), 0)
+        found = jnp.dot(left, jnp.concatenate([hot, hot], axis=0), preferred_element_type=jnp.float32)
+        chosen = jnp.concatenate([spot == spot_lines[j:j + 1] for j in range(lines)], axis=1)
+        parts = [jnp.sum(jnp.where(chosen, found[p * spots:(p + 1) * spots], 0.0), axis=0, keepdims=True) for p in range(2)]
         return jnp.concatenate(parts, axis=0)
 
     def remote(dest):
         return pltpu.make_async_remote_copy(
             src_ref=outgoing.at[dest],
             dst_ref=incoming.at[me],
-            send_sem=send_sems.at[dest],
-            recv_sem=recv_sems.at[me],
+            send_sem=send_sem,
+            recv_sem=recv_sem,
             device_id={"cuts": dest},
             device_id_type=pl.DeviceIdType.MESH,
         )
 
     def serve(start, count):
-        dests = [lax.rem(me + 1 + start + i, n) for i in range(count)]
+        dests = [nth_dest(start + i) for i in range(count)]
         for i, dest in enumerate(dests):
             hot = hot_v[start + i] if hot_v.shape[0] == n else hot_columns(dest)
             outgoing[dest, :, :mine] = picked(dest, hot)
@@ -143,19 +154,9 @@
     incoming[me, :, :mine] = picked(me, hot_v[n - 1] if hot_v.shape[0] == n else hot_columns(me))
     incoming[me, :, mine:] = stats
 
-    def receive(k, carry):
-        source = lax.rem(me + k, n)
-        pltpu.make_async_remote_copy(
-            src_ref=outgoing.at[source],
-            dst_ref=incoming.at[source],
-            send_sem=send_sems.at[source],
-            recv_sem=recv_sems.at[source],
-            device_id={"cuts": source},
-            device_id_type=pl.DeviceIdType.MESH,
-        ).wait()
-        return carry
-
-    lax.fori_loop(1, n, receive, 0)
+    everything = pl.ds(0, n - 1)
+    pltpu.make_async_copy(outgoing.at[everything], incoming.at[everything], recv_sem).wait()
+    pltpu.make_async_copy(outgoing.at[everything], incoming.at[everything], send_sem).wait()
     out_ref[:, :mine] = jnp.sum(incoming[:, :, :mine], axis=0)
     out_ref[:, mine:] = jnp.max(incoming[:, :, mine:], axis=0)
 
@@ -180,7 +181,6 @@
     slices = stem_tensor.shape[1]
     mine = bit_rows.shape[0] // n
     steps = branch_tensors.shape[0]
-    width = stem_tensor.shape[3]
     any_spec = pl.BlockSpec(memory_space=pl.ANY)
     lined = (n, mine // LANES, LANES)
     sums = pl.pallas_call(
@@ -195,12 +195,12 @@
             pltpu.VMEM(branch_tensors.shape[1:], jnp.bfloat16),
             pltpu.VMEM(lined, jnp.int32),
             pltpu.VMEM(lined, jnp.int32),
-            pltpu.VMEM((n if n <= 16 else 1, width, mine), jnp.bfloat16),
+            pltpu.VMEM((n if n <= 16 else 1, LANES, mine), jnp.bfloat16),
             pltpu.VMEM((n, 2, mine + LANES), jnp.float32),
             pltpu.VMEM((n, 2, mine + LANES), jnp.float32),
             pltpu.SemaphoreType.DMA((4 + 4 * steps,)),
-            pltpu.SemaphoreType.DMA((n,)),
-            pltpu.SemaphoreType.DMA((n,)),
+            pltpu.SemaphoreType.DMA,
+            pltpu.SemaphoreType.DMA,
         ],
         compiler_params=pltpu.CompilerParams(
             collective_id=0, has_side_effects=True, vmem_limit_bytes=56 * 1024 * 1024

time: 13.5 us -> 14.4 us (1.067)
  Pallas kernels: 12.7 us -> 13.7 us
    pallas_call x1, Pallas kernels: 12.1 us -> 13 us  [shards(): pl.pallas_call(functools.partial(kernel, n, 3), out_shape=pltpu.VMEM((2,...]
where the time goes in v4:
time: 14.4 us; the launch traced here: 14.3 us
  Pallas kernels  13.7 us (95%)
  between operations  0.64 us (4%)
    pallas_call x1, Pallas kernels, shards(): pl.pallas_call(functools.partial(kernel, n, 3), out_shape=pltpu.VMEM((2,...  13 us
    pallas_call x1, Pallas kernels, shards(): pl.pallas_call(finish, out_shape=(jax.ShapeDtypeStruct((2, mine), jnp.flo...  0.67 us

profile of v4, /device:TPU:0, one launch (start us, length us, event | category | flops | bytes accessed | tf_op | source)
XLA Modules:
  0.0 14.3 jit_solution(7893770130280816734)
XLA Ops:
  0.6 13.0 %shard_map.68.sum_ref = f32[2,640]{1,0:T(2,128)S(1)} custom-call(s32[2,4]{1,0:T(2,128)} %bitcast.6, bf16[2,4,32,512]{3,2,1,0:T(8,128)(2,1)} %stem_hbm.1, bf16[2,2,2,512,512]{4,3,2,1,0:T(8,128)(2,1)} %branch_hbm.1, s32[16,4,128]{2,1,0:T(4,128)} %bitcast.4, s32[16,4,128]{2,1,0:T(4,128)} %bitcast.5), custom_call_target="tpu_custom_call" | custom-call | tf_op jit(solution)/shard_map/pallas_call | solution.py:186
  13.6 0.7 %shard_map.69 = (f32[2,512]{1,0:T(2,128)}, f32[1,1]{1,0:T(1,128)}) custom-call(f32[2,640]{1,0:T(2,128)S(1)} %shard_map.68.sum_ref), custom_call_target="tpu_custom_call" | custom-call | tf_op jit(solution)/shard_map/pallas_call | solution.py:209

commit v5 on v4

--- a/solution.py
+++ b/solution.py
@@ -61,8 +61,7 @@
         return jnp.concatenate([jnp.where(column == line, one, zero) for line in lanes], axis=1)
 
     def nth_dest(i):
-        swing = (i + 1) // 2
-        return lax.rem(me + n // 2 + swing * (1 - 2 * (i % 2)) + n, n)
+        return jnp.where(i >= n - 1, me, jnp.where(i >= me, i + 1, i))
 
     def keep_hot(i, carry):
         hot_v[i] = hot_columns(nth_dest(i))
@@ -184,7 +183,7 @@
     any_spec = pl.BlockSpec(memory_space=pl.ANY)
     lined = (n, mine // LANES, LANES)
     sums = pl.pallas_call(
-        functools.partial(kernel, n, 3),
+        functools.partial(kernel, n, 2),
         out_shape=pltpu.VMEM((2, mine + LANES), jnp.float32),
         in_specs=[any_spec] * 5,
         out_specs=pl.BlockSpec(memory_space=pltpu.VMEM),

time: 14.4 us -> 13 us (0.903)
  Pallas kernels: 13.7 us -> 12.2 us
    pallas_call x1, Pallas kernels: 13 us -> 11.5 us  [shards(): pl.pallas_call(functools.partial(kernel, n, 2), out_shape=pltpu.VMEM((2,...]
where the time goes in v5:
time: 13 us; the launch traced here: 12.8 us
  Pallas kernels  12.2 us (94%)
  between operations  0.64 us (5%)
    pallas_call x1, Pallas kernels, shards(): pl.pallas_call(functools.partial(kernel, n, 2), out_shape=pltpu.VMEM((2,...  11.5 us
    pallas_call x1, Pallas kernels, shards(): pl.pallas_call(finish, out_shape=(jax.ShapeDtypeStruct((2, mine), jnp.flo...  0.67 us

profile of v5, /device:TPU:0, one launch (start us, length us, event | category | flops | bytes accessed | tf_op | source)
XLA Modules:
  0.0 12.8 jit_solution(15696976974505659426)
XLA Ops:
  0.6 11.5 %shard_map.68.sum_ref = f32[2,640]{1,0:T(2,128)S(1)} custom-call(s32[2,4]{1,0:T(2,128)} %bitcast.6, bf16[2,4,32,512]{3,2,1,0:T(8,128)(2,1)} %stem_hbm.1, bf16[2,2,2,512,512]{4,3,2,1,0:T(8,128)(2,1)} %branch_hbm.1, s32[16,4,128]{2,1,0:T(4,128)} %bitcast.4, s32[16,4,128]{2,1,0:T(4,128)} %bitcast.5), custom_call_target="tpu_custom_call" | custom-call | tf_op jit(solution)/shard_map/pallas_call | solution.py:185
  12.2 0.7 %shard_map.69 = (f32[2,512]{1,0:T(2,128)}, f32[1,1]{1,0:T(1,128)}) custom-call(f32[2,640]{1,0:T(2,128)S(1)} %shard_map.68.sum_ref), custom_call_target="tpu_custom_call" | custom-call | tf_op jit(solution)/shard_map/pallas_call | solution.py:208

commit v6 on v5

--- a/solution.py
+++ b/solution.py
@@ -11,11 +11,18 @@
 LIFT = 2.0 ** 20
 
 
-def complex_step(real_part, imag_part, weights):
-    upper = jnp.concatenate([real_part, -imag_part], axis=1)
-    lower = jnp.concatenate([imag_part, real_part], axis=1)
-    left = jnp.concatenate([upper, lower], axis=0)
-    return jnp.dot(left, weights, preferred_element_type=jnp.float32)
+def complex_step(parts, flags, matrices):
+    rows = []
+    for (real_part, imag_part), flag in zip(parts, flags):
+        real_parts = [real_part * f for f in flag]
+        imag_parts = [imag_part * f for f in flag]
+        for signed in ([[r, -i] for r, i in zip(real_parts, imag_parts)], [[i, r] for r, i in zip(real_parts, imag_parts)]):
+            rows.append(jnp.concatenate([x.astype(jnp.bfloat16) for pair in signed for x in pair], axis=1))
+    left = jnp.concatenate(rows, axis=0)
+    values, kinds, depth, width = matrices.shape
+    found = jnp.dot(left, matrices.reshape(values * kinds * depth, width), preferred_element_type=jnp.float32)
+    height = found.shape[0] // len(parts)
+    return [found[s * height:(s + 1) * height] for s in range(len(parts))]
 
 
 def largest(values):
@@ -75,17 +82,17 @@
     stem_load.wait()
     for load in branch_loads[0]:
         load.wait()
-    first = []
-    for s in range(slices):
-        weights = early_v[cut_s[0, s]].reshape(2 * width, width)
-        first.append(complex_step(stem_v[0, s], stem_v[1, s], weights))
+    def flags(step, scale, dtype):
+        return [
+            [jnp.full((1, 1), jnp.where(cut_s[step, s] == v, scale, 0.0)).astype(dtype) for v in range(2)]
+            for s in range(slices)
+        ]
+
+    first = complex_step(
+        [(stem_v[0, s], stem_v[1, s]) for s in range(slices)], flags(0, 1.0, jnp.bfloat16), early_v[...])
     for load in branch_loads[1]:
         load.wait()
-    second = []
-    for s in range(slices):
-        state = (first[s] * LIFT).astype(jnp.bfloat16)
-        weights = later_v[cut_s[1, s]].reshape(2 * width, width)
-        second.append(complex_step(state[:rows], state[rows:], weights))
+    second = complex_step([(p[:rows], p[rows:]) for p in first], flags(1, LIFT, jnp.float32), later_v[...])
 
     square = functools.reduce(jnp.maximum, [p[:rows] * p[:rows] + p[rows:] * p[rows:] for p in first])
     peak_square = largest(square)

time: 13 us -> 12.7 us (0.977)
  Pallas kernels: 12.2 us -> 11.9 us
    pallas_call x1, Pallas kernels: 11.5 us -> 11.3 us  [shards(): pl.pallas_call(functools.partial(kernel, n, 2), out_shape=pltpu.VMEM((2,...]
where the time goes in v6:
time: 12.7 us; the launch traced here: 12.6 us
  Pallas kernels  11.9 us (94%)
  between operations  0.64 us (5%)
    pallas_call x1, Pallas kernels, shards(): pl.pallas_call(functools.partial(kernel, n, 2), out_shape=pltpu.VMEM((2,...  11.3 us
    pallas_call x1, Pallas kernels, shards(): pl.pallas_call(finish, out_shape=(jax.ShapeDtypeStruct((2, mine), jnp.flo...  0.67 us

profile of v6, /device:TPU:0, one launch (start us, length us, event | category | flops | bytes accessed | tf_op | source)
XLA Modules:
  0.0 12.6 jit_solution(13779214077467743616)
XLA Ops:
  0.6 11.3 %shard_map.68.sum_ref = f32[2,640]{1,0:T(2,128)S(1)} custom-call(s32[2,4]{1,0:T(2,128)} %bitcast.6, bf16[2,4,32,512]{3,2,1,0:T(8,128)(2,1)} %stem_hbm.1, bf16[2,2,2,512,512]{4,3,2,1,0:T(8,128)(2,1)} %branch_hbm.1, s32[16,4,128]{2,1,0:T(4,128)} %bitcast.4, s32[16,4,128]{2,1,0:T(4,128)} %bitcast.5), custom_call_target="tpu_custom_call" | custom-call | tf_op jit(solution)/shard_map/pallas_call | solution.py:192
  11.9 0.7 %shard_map.69 = (f32[2,512]{1,0:T(2,128)}, f32[1,1]{1,0:T(1,128)}) custom-call(f32[2,640]{1,0:T(2,128)S(1)} %shard_map.68.sum_ref), custom_call_target="tpu_custom_call" | custom-call | tf_op jit(solution)/shard_map/pallas_call | solution.py:215

commit v7 on v6

--- a/solution.py
+++ b/solution.py
@@ -11,16 +11,21 @@
 LIFT = 2.0 ** 20
 
 
-def complex_step(parts, flags, matrices):
-    rows = []
-    for (real_part, imag_part), flag in zip(parts, flags):
-        real_parts = [real_part * f for f in flag]
-        imag_parts = [imag_part * f for f in flag]
-        for signed in ([[r, -i] for r, i in zip(real_parts, imag_parts)], [[i, r] for r, i in zip(real_parts, imag_parts)]):
-            rows.append(jnp.concatenate([x.astype(jnp.bfloat16) for pair in signed for x in pair], axis=1))
-    left = jnp.concatenate(rows, axis=0)
-    values, kinds, depth, width = matrices.shape
-    found = jnp.dot(left, matrices.reshape(values * kinds * depth, width), preferred_element_type=jnp.float32)
+def complex_step(parts, flags, matrices, loads):
+    found = None
+    for v in range(matrices.shape[0]):
+        rows = []
+        for (real_part, imag_part), flag in zip(parts, flags):
+            real_now = real_part * flag[v]
+            imag_now = imag_part * flag[v]
+            for pair in ((real_now, -imag_now), (imag_now, real_now)):
+                rows.append(jnp.concatenate([x.astype(jnp.bfloat16) for x in pair], axis=1))
+        left = jnp.concatenate(rows, axis=0)
+        for load in loads[v]:
+            load.wait()
+        _, kinds, depth, width = matrices.shape
+        product = jnp.dot(left, matrices[v].reshape(kinds * depth, width), preferred_element_type=jnp.float32)
+        found = product if found is None else found + product
     height = found.shape[0] // len(parts)
     return [found[s * height:(s + 1) * height] for s in range(len(parts))]
 
@@ -30,7 +35,7 @@
 
 
 def kernel(n, group, cut_hbm, stem_hbm, branch_hbm, rows_hbm, cols_hbm, out_ref,
-           cut_s, stem_v, early_v, later_v, rows_v, cols_v, hot_v, outgoing, incoming, load_sems, send_sem, recv_sem):
+           cut_s, stem_v, early_v, later_v, rows_v, cols_v, outgoing, incoming, load_sems, send_sem, recv_sem):
     me = lax.axis_index("cuts")
     slices, rows, width = stem_hbm.shape[1], stem_hbm.shape[2], stem_hbm.shape[3]
     mine = out_ref.shape[1] - LANES
@@ -42,13 +47,17 @@
     stem_load = pltpu.make_async_copy(stem_hbm, stem_v, load_sems.at[3])
     branch_loads = [
         [
-            pltpu.make_async_copy(
-                branch_hbm.at[step, value, part], held.at[value, part], load_sems.at[4 + 4 * step + 2 * value + part])
-            for value in range(2) for part in range(2)
+            [
+                pltpu.make_async_copy(
+                    branch_hbm.at[step, value, part], held.at[value, part], load_sems.at[4 + 4 * step + 2 * value + part])
+                for part in range(2)
+            ]
+            for value in range(2)
         ]
         for step, held in enumerate((early_v, later_v))
     ]
-    for load in [cols_load, stem_load, cut_load] + branch_loads[0] + [rows_load] + branch_loads[1]:
+    for load in [cut_load, stem_load, *branch_loads[0][0], *branch_loads[0][1], cols_load, rows_load,
+                 *branch_loads[1][0], *branch_loads[1][1]]:
         load.start()
 
     barrier = pltpu.get_barrier_semaphore()
@@ -70,18 +79,8 @@
     def nth_dest(i):
         return jnp.where(i >= n - 1, me, jnp.where(i >= me, i + 1, i))
 
-    def keep_hot(i, carry):
-        hot_v[i] = hot_columns(nth_dest(i))
-        return carry
-
-    cols_load.wait()
-    if hot_v.shape[0] == n:
-        lax.fori_loop(0, n, keep_hot, 0)
-
     cut_load.wait()
     stem_load.wait()
-    for load in branch_loads[0]:
-        load.wait()
     def flags(step, scale, dtype):
         return [
             [jnp.full((1, 1), jnp.where(cut_s[step, s] == v, scale, 0.0)).astype(dtype) for v in range(2)]
@@ -89,10 +88,12 @@
         ]
 
     first = complex_step(
-        [(stem_v[0, s], stem_v[1, s]) for s in range(slices)], flags(0, 1.0, jnp.bfloat16), early_v[...])
-    for load in branch_loads[1]:
+        [(stem_v[0, s], stem_v[1, s]) for s in range(slices)], flags(0, 1.0, jnp.bfloat16), early_v, branch_loads[0])
+    cols_load.wait()
+    rows_load.wait()
+    for load in branch_loads[1][0] + branch_loads[1][1]:
         load.wait()
-    second = complex_step([(p[:rows], p[rows:]) for p in first], flags(1, LIFT, jnp.float32), later_v[...])
+    second = complex_step([(p[:rows], p[rows:]) for p in first], flags(1, LIFT, jnp.float32), later_v, [[], []])
 
     square = functools.reduce(jnp.maximum, [p[:rows] * p[:rows] + p[rows:] * p[rows:] for p in first])
     peak_square = largest(square)
@@ -115,10 +116,8 @@
 
     left = jnp.concatenate([blocked(high), blocked(low)], axis=1)
 
-    rows_load.wait()
-    pl.semaphore_wait(barrier, n - 1)
-
-    def picked(dest, hot):
+    def picked(dest):
+        hot = hot_columns(dest)
         spots = blocks * rows
         spot_lines = (cols_v[dest] // LANES) * rows + rows_v[dest]
         spot = lax.broadcasted_iota(jnp.int32, (spots, LANES), 0)
@@ -139,10 +138,11 @@
 
     def serve(start, count):
         dests = [nth_dest(start + i) for i in range(count)]
-        for i, dest in enumerate(dests):
-            hot = hot_v[start + i] if hot_v.shape[0] == n else hot_columns(dest)
-            outgoing[dest, :, :mine] = picked(dest, hot)
+        for dest in dests:
+            outgoing[dest, :, :mine] = picked(dest)
             outgoing[dest, :, mine:] = stats
+        if isinstance(start, int) and start == 0:
+            pl.semaphore_wait(barrier, n - 1)
         for dest in dests:
             remote(dest).start()
 
@@ -150,14 +150,15 @@
         serve(g * group, group)
         return carry
 
+    serve(0, group)
     rounds = (n - 1) // group
-    if hot_v.shape[0] == n:
-        for g in range(rounds):
+    if n <= 16:
+        for g in range(1, rounds):
             serve(g * group, group)
     else:
-        lax.fori_loop(0, rounds, serve_group, 0)
+        lax.fori_loop(1, rounds, serve_group, 0)
     serve(rounds * group, n - 1 - rounds * group)
-    incoming[me, :, :mine] = picked(me, hot_v[n - 1] if hot_v.shape[0] == n else hot_columns(me))
+    incoming[me, :, :mine] = picked(me)
     incoming[me, :, mine:] = stats
 
     everything = pl.ds(0, n - 1)
@@ -201,7 +202,6 @@
             pltpu.VMEM(branch_tensors.shape[1:], jnp.bfloat16),
             pltpu.VMEM(lined, jnp.int32),
             pltpu.VMEM(lined, jnp.int32),
-            pltpu.VMEM((n if n <= 16 else 1, LANES, mine), jnp.bfloat16),
             pltpu.VMEM((n, 2, mine + LANES), jnp.float32),
             pltpu.VMEM((n, 2, mine + LANES), jnp.float32),
             pltpu.SemaphoreType.DMA((4 + 4 * steps,)),

time: 12.7 us -> 12.6 us (level)
    pallas_call x1, Pallas kernels: 11.3 us -> 11.1 us  [shards(): pl.pallas_call(functools.partial(kernel, n, 2), out_shape=pltpu.VMEM((2,...]
where the time goes in v7:
time: 12.6 us; the launch traced here: 12.4 us
  Pallas kernels  11.8 us (94%)
  between operations  0.64 us (5%)
    pallas_call x1, Pallas kernels, shards(): pl.pallas_call(functools.partial(kernel, n, 2), out_shape=pltpu.VMEM((2,...  11.1 us
    pallas_call x1, Pallas kernels, shards(): pl.pallas_call(finish, out_shape=(jax.ShapeDtypeStruct((2, mine), jnp.flo...  0.67 us

profile of v7, /device:TPU:0, one launch (start us, length us, event | category | flops | bytes accessed | tf_op | source)
XLA Modules:
  0.0 12.4 jit_solution(6646616927985073313)
XLA Ops:
  0.6 11.1 %shard_map.68.sum_ref = f32[2,640]{1,0:T(2,128)S(1)} custom-call(s32[2,4]{1,0:T(2,128)} %bitcast.6, bf16[2,4,32,512]{3,2,1,0:T(8,128)(2,1)} %stem_hbm.1, bf16[2,2,2,512,512]{4,3,2,1,0:T(8,128)(2,1)} %branch_hbm.1, s32[16,4,128]{2,1,0:T(4,128)} %bitcast.4, s32[16,4,128]{2,1,0:T(4,128)} %bitcast.5), custom_call_target="tpu_custom_call" | custom-call | tf_op jit(solution)/shard_map/pallas_call | solution.py:193
  11.8 0.7 %shard_map.69 = (f32[2,512]{1,0:T(2,128)}, f32[1,1]{1,0:T(1,128)}) custom-call(f32[2,640]{1,0:T(2,128)S(1)} %shard_map.68.sum_ref), custom_call_target="tpu_custom_call" | custom-call | tf_op jit(solution)/shard_map/pallas_call | solution.py:215

commit v8 on v7

--- a/solution.py
+++ b/solution.py
@@ -19,7 +19,7 @@
             real_now = real_part * flag[v]
             imag_now = imag_part * flag[v]
             for pair in ((real_now, -imag_now), (imag_now, real_now)):
-                rows.append(jnp.concatenate([x.astype(jnp.bfloat16) for x in pair], axis=1))
+                rows.append(jnp.concatenate(pair, axis=1))
         left = jnp.concatenate(rows, axis=0)
         for load in loads[v]:
             load.wait()
@@ -81,19 +81,17 @@
 
     cut_load.wait()
     stem_load.wait()
-    def flags(step, scale, dtype):
+    def flags(step):
         return [
-            [jnp.full((1, 1), jnp.where(cut_s[step, s] == v, scale, 0.0)).astype(dtype) for v in range(2)]
+            [jnp.full((1, 1), jnp.where(cut_s[step, s] == v, 1.0, 0.0)).astype(jnp.bfloat16) for v in range(2)]
             for s in range(slices)
         ]
 
-    first = complex_step(
-        [(stem_v[0, s], stem_v[1, s]) for s in range(slices)], flags(0, 1.0, jnp.bfloat16), early_v, branch_loads[0])
+    first = complex_step([(stem_v[0, s], stem_v[1, s]) for s in range(slices)], flags(0), early_v, branch_loads[0])
     cols_load.wait()
     rows_load.wait()
-    for load in branch_loads[1][0] + branch_loads[1][1]:
-        load.wait()
-    second = complex_step([(p[:rows], p[rows:]) for p in first], flags(1, LIFT, jnp.float32), later_v, [[], []])
+    states = [(p * LIFT).astype(jnp.bfloat16) for p in first]
+    second = complex_step([(p[:rows], p[rows:]) for p in states], flags(1), later_v, branch_loads[1])
 
     square = functools.reduce(jnp.maximum, [p[:rows] * p[:rows] + p[rows:] * p[rows:] for p in first])
     peak_square = largest(square)
@@ -147,17 +145,18 @@
             remote(dest).start()
 
     def serve_group(g, carry):
-        serve(g * group, group)
+        serve(2 + g * group, group)
         return carry
 
-    serve(0, group)
-    rounds = (n - 1) // group
+    serve(0, 1)
+    serve(1, 1)
+    rounds = (n - 3) // group
     if n <= 16:
-        for g in range(1, rounds):
-            serve(g * group, group)
+        for g in range(rounds):
+            serve(2 + g * group, group)
     else:
-        lax.fori_loop(1, rounds, serve_group, 0)
-    serve(rounds * group, n - 1 - rounds * group)
+        lax.fori_loop(0, rounds, serve_group, 0)
+    serve(2 + rounds * group, n - 3 - rounds * group)
     incoming[me, :, :mine] = picked(me)
     incoming[me, :, mine:] = stats
 

time: 12.6 us -> 12.6 us (level)
  no operation moved by 1% of the time
where the time goes in v8:
time: 12.6 us; the launch traced here: 12.5 us
  Pallas kernels  11.8 us (94%)
  between operations  0.64 us (5%)
    pallas_call x1, Pallas kernels, shards(): pl.pallas_call(functools.partial(kernel, n, 2), out_shape=pltpu.VMEM((2,...  11.2 us
    pallas_call x1, Pallas kernels, shards(): pl.pallas_call(finish, out_shape=(jax.ShapeDtypeStruct((2, mine), jnp.flo...  0.67 us

profile of v8, /device:TPU:0, one launch (start us, length us, event | category | flops | bytes accessed | tf_op | source)
XLA Modules:
  0.0 12.5 jit_solution(3809425356464969888)
XLA Ops:
  0.6 11.2 %shard_map.68.sum_ref = f32[2,640]{1,0:T(2,128)S(1)} custom-call(s32[2,4]{1,0:T(2,128)} %bitcast.6, bf16[2,4,32,512]{3,2,1,0:T(8,128)(2,1)} %stem_hbm.1, bf16[2,2,2,512,512]{4,3,2,1,0:T(8,128)(2,1)} %branch_hbm.1, s32[16,4,128]{2,1,0:T(4,128)} %bitcast.4, s32[16,4,128]{2,1,0:T(4,128)} %bitcast.5), custom_call_target="tpu_custom_call" | custom-call | tf_op jit(solution)/shard_map/pallas_call | solution.py:192
  11.8 0.7 %shard_map.69 = (f32[2,512]{1,0:T(2,128)}, f32[1,1]{1,0:T(1,128)}) custom-call(f32[2,640]{1,0:T(2,128)S(1)} %shard_map.68.sum_ref), custom_call_target="tpu_custom_call" | custom-call | tf_op jit(solution)/shard_map/pallas_call | solution.py:214

commit v9 on v7

--- a/solution.py
+++ b/solution.py
@@ -136,30 +136,41 @@
             device_id_type=pl.DeviceIdType.MESH,
         )
 
+    def fill(dest):
+        outgoing[dest, :, :mine] = picked(dest)
+        outgoing[dest, :, mine:] = stats
+
     def serve(start, count):
         dests = [nth_dest(start + i) for i in range(count)]
         for dest in dests:
-            outgoing[dest, :, :mine] = picked(dest)
-            outgoing[dest, :, mine:] = stats
+            fill(dest)
         if isinstance(start, int) and start == 0:
             pl.semaphore_wait(barrier, n - 1)
         for dest in dests:
             remote(dest).start()
 
-    def serve_group(g, carry):
-        serve(g * group, group)
-        return carry
-
-    serve(0, group)
-    rounds = (n - 1) // group
-    if n <= 16:
-        for g in range(1, rounds):
-            serve(g * group, group)
-    else:
-        lax.fori_loop(1, rounds, serve_group, 0)
-    serve(rounds * group, n - 1 - rounds * group)
-    incoming[me, :, :mine] = picked(me)
-    incoming[me, :, mine:] = stats
+    def keep_own():
+        incoming[me, :, :mine] = picked(me)
+        incoming[me, :, mine:] = stats
+
+    @pl.when(me < n // 2)
+    def _():
+        lax.fori_loop(0, n - 1, lambda i, carry: (fill(nth_dest(i)), carry)[1], 0)
+        keep_own()
+        pl.semaphore_wait(barrier, n - 1)
+        lax.fori_loop(0, n - 1, lambda i, carry: (remote(nth_dest(i)).start(), carry)[1], 0)
+
+    @pl.when(me >= n // 2)
+    def _():
+        serve(0, group)
+        rounds = (n - 1) // group
+        if n <= 16:
+            for g in range(1, rounds):
+                serve(g * group, group)
+        else:
+            lax.fori_loop(1, rounds, lambda g, carry: (serve(g * group, group), carry)[1], 0)
+        serve(rounds * group, n - 1 - rounds * group)
+        keep_own()
 
     everything = pl.ds(0, n - 1)
     pltpu.make_async_copy(outgoing.at[everything], incoming.at[everything], recv_sem).wait()

time: 12.6 us -> 14.5 us (1.15)
  Pallas kernels: 11.8 us -> 13.7 us
    pallas_call x1, Pallas kernels: 11.1 us -> 13 us  [shards(): pl.pallas_call(functools.partial(kernel, n, 2), out_shape=pltpu.VMEM((2,...]
where the time goes in v9:
time: 14.5 us; the launch traced here: 14.3 us
  Pallas kernels  13.7 us (94%)
  between operations  0.64 us (4%)
    pallas_call x1, Pallas kernels, shards(): pl.pallas_call(functools.partial(kernel, n, 2), out_shape=pltpu.VMEM((2,...  13 us
    pallas_call x1, Pallas kernels, shards(): pl.pallas_call(finish, out_shape=(jax.ShapeDtypeStruct((2, mine), jnp.flo...  0.67 us

profile of v9, /device:TPU:0, one launch (start us, length us, event | category | flops | bytes accessed | tf_op | source)
XLA Modules:
  0.0 14.3 jit_solution(14987072199417850466)
XLA Ops:
  0.6 13.0 %shard_map.68.sum_ref = f32[2,640]{1,0:T(2,128)S(1)} custom-call(s32[2,4]{1,0:T(2,128)} %bitcast.6, bf16[2,4,32,512]{3,2,1,0:T(8,128)(2,1)} %stem_hbm.1, bf16[2,2,2,512,512]{4,3,2,1,0:T(8,128)(2,1)} %branch_hbm.1, s32[16,4,128]{2,1,0:T(4,128)} %bitcast.4, s32[16,4,128]{2,1,0:T(4,128)} %bitcast.5), custom_call_target="tpu_custom_call" | custom-call | tf_op jit(solution)/shard_map/pallas_call | solution.py:204
  13.6 0.7 %shard_map.69 = (f32[2,512]{1,0:T(2,128)}, f32[1,1]{1,0:T(1,128)}) custom-call(f32[2,640]{1,0:T(2,128)S(1)} %shard_map.68.sum_ref), custom_call_target="tpu_custom_call" | custom-call | tf_op jit(solution)/shard_map/pallas_call | solution.py:226

commit v10 on v7

--- a/solution.py
+++ b/solution.py
@@ -8,6 +8,7 @@
 from jax.sharding import PartitionSpec as P
 
 LANES = 128
+DEPTH = 256
 LIFT = 2.0 ** 20
 
 
@@ -70,10 +71,10 @@
 
     def hot_columns(dest):
         col_lines = cols_v[dest]
-        column = lax.broadcasted_iota(jnp.int16, (LANES, LANES), 0)
+        column = lax.broadcasted_iota(jnp.int16, (DEPTH, LANES), 0)
         one, zero = jnp.bfloat16(1), jnp.bfloat16(0)
-        low_part = lax.rem(col_lines, LANES)
-        lanes = [jnp.broadcast_to(low_part[j:j + 1], (LANES, LANES)).astype(jnp.int16) for j in range(lines)]
+        low_part = lax.rem(col_lines, DEPTH)
+        lanes = [jnp.broadcast_to(low_part[j:j + 1], (DEPTH, LANES)).astype(jnp.int16) for j in range(lines)]
         return jnp.concatenate([jnp.where(column == line, one, zero) for line in lanes], axis=1)
 
     def nth_dest(i):
@@ -106,22 +107,17 @@
         [jnp.broadcast_to(peak_square, (1, LANES)), jnp.broadcast_to(raw_second, (1, LANES))], axis=0)
 
     table = functools.reduce(jnp.add, second)
-    high = table.astype(jnp.bfloat16)
-    low = (table - high.astype(jnp.float32)).astype(jnp.bfloat16)
-    blocks = width // LANES
-
-    def blocked(half):
-        return jnp.concatenate(
-            [half[p * rows:(p + 1) * rows, c * LANES:(c + 1) * LANES] for p in range(2) for c in range(blocks)], axis=0)
-
-    left = jnp.concatenate([blocked(high), blocked(low)], axis=1)
+    rounded = table.astype(jnp.bfloat16)
+    blocks = width // DEPTH
+    left = jnp.concatenate(
+        [rounded[p * rows:(p + 1) * rows, c * DEPTH:(c + 1) * DEPTH] for p in range(2) for c in range(blocks)], axis=0)
 
     def picked(dest):
         hot = hot_columns(dest)
         spots = blocks * rows
-        spot_lines = (cols_v[dest] // LANES) * rows + rows_v[dest]
+        spot_lines = (cols_v[dest] // DEPTH) * rows + rows_v[dest]
         spot = lax.broadcasted_iota(jnp.int32, (spots, LANES), 0)
-        found = jnp.dot(left, jnp.concatenate([hot, hot], axis=0), preferred_element_type=jnp.float32)
+        found = jnp.dot(left, hot, preferred_element_type=jnp.float32)
         chosen = jnp.concatenate([spot == spot_lines[j:j + 1] for j in range(lines)], axis=1)
         parts = [jnp.sum(jnp.where(chosen, found[p * spots:(p + 1) * spots], 0.0), axis=0, keepdims=True) for p in range(2)]
         return jnp.concatenate(parts, axis=0)
@@ -146,18 +142,14 @@
         for dest in dests:
             remote(dest).start()
 
-    def serve_group(g, carry):
-        serve(g * group, group)
-        return carry
-
-    serve(0, group)
-    rounds = (n - 1) // group
+    head = (n - 2) % group + 1
+    rounds = (n - 1 - head) // group
+    serve(0, head)
     if n <= 16:
-        for g in range(1, rounds):
-            serve(g * group, group)
+        for g in range(rounds):
+            serve(head + g * group, group)
     else:
-        lax.fori_loop(1, rounds, serve_group, 0)
-    serve(rounds * group, n - 1 - rounds * group)
+        lax.fori_loop(0, rounds, lambda g, carry: (serve(head + g * group, group), carry)[1], 0)
     incoming[me, :, :mine] = picked(me)
     incoming[me, :, mine:] = stats
 
@@ -191,7 +183,7 @@
     any_spec = pl.BlockSpec(memory_space=pl.ANY)
     lined = (n, mine // LANES, LANES)
     sums = pl.pallas_call(
-        functools.partial(kernel, n, 2),
+        functools.partial(kernel, n, 4),
         out_shape=pltpu.VMEM((2, mine + LANES), jnp.float32),
         in_specs=[any_spec] * 5,
         out_specs=pl.BlockSpec(memory_space=pltpu.VMEM),

time: 12.6 us -> 12.6 us (level)
  no operation moved by 1% of the time
where the time goes in v10:
time: 12.6 us; the launch traced here: 12.4 us
  Pallas kernels  11.8 us (94%)
  between operations  0.64 us (5%)
    pallas_call x1, Pallas kernels, shards(): pl.pallas_call(functools.partial(kernel, n, 4), out_shape=pltpu.VMEM((2,...  11.1 us
    pallas_call x1, Pallas kernels, shards(): pl.pallas_call(finish, out_shape=(jax.ShapeDtypeStruct((2, mine), jnp.flo...  0.67 us

profile of v10, /device:TPU:0, one launch (start us, length us, event | category | flops | bytes accessed | tf_op | source)
XLA Modules:
  0.0 12.4 jit_solution(11168317603794679531)
XLA Ops:
  0.6 11.1 %shard_map.68.sum_ref = f32[2,640]{1,0:T(2,128)S(1)} custom-call(s32[2,4]{1,0:T(2,128)} %bitcast.6, bf16[2,4,32,512]{3,2,1,0:T(8,128)(2,1)} %stem_hbm.1, bf16[2,2,2,512,512]{4,3,2,1,0:T(8,128)(2,1)} %branch_hbm.1, s32[16,4,128]{2,1,0:T(4,128)} %bitcast.4, s32[16,4,128]{2,1,0:T(4,128)} %bitcast.5), custom_call_target="tpu_custom_call" | custom-call | tf_op jit(solution)/shard_map/pallas_call | solution.py:185
  11.8 0.7 %shard_map.69 = (f32[2,512]{1,0:T(2,128)}, f32[1,1]{1,0:T(1,128)}) custom-call(f32[2,640]{1,0:T(2,128)S(1)} %shard_map.68.sum_ref), custom_call_target="tpu_custom_call" | custom-call | tf_op jit(solution)/shard_map/pallas_call | solution.py:207

commit v11 on v10

--- a/solution.py
+++ b/solution.py
@@ -46,12 +46,15 @@
     rows_load = pltpu.make_async_copy(rows_hbm, rows_v, load_sems.at[1])
     cut_load = pltpu.make_async_copy(cut_hbm, cut_s, load_sems.at[2])
     stem_load = pltpu.make_async_copy(stem_hbm, stem_v, load_sems.at[3])
+    half = width // 2
     branch_loads = [
         [
             [
                 pltpu.make_async_copy(
-                    branch_hbm.at[step, value, part], held.at[value, part], load_sems.at[4 + 4 * step + 2 * value + part])
-                for part in range(2)
+                    branch_hbm.at[step, value, part, pl.ds(start, half)],
+                    held.at[value, part, pl.ds(start, half)],
+                    load_sems.at[4 + 8 * step + 4 * value + 2 * part + start // half])
+                for part in range(2) for start in (0, half)
             ]
             for value in range(2)
         ]
@@ -67,7 +70,7 @@
         pl.semaphore_signal(barrier, inc=1, device_id={"cuts": lax.rem(me + k, n)}, device_id_type=pl.DeviceIdType.MESH)
         return carry
 
-    lax.fori_loop(1, n, greet, 0)
+    lax.fori_loop(1, n, greet, 0, unroll=n <= 16)
 
     def hot_columns(dest):
         col_lines = cols_v[dest]
@@ -142,9 +145,10 @@
         for dest in dests:
             remote(dest).start()
 
-    head = (n - 2) % group + 1
+    serve(0, 1)
+    head = 1 + (n - 2) % group
+    serve(1, head - 1)
     rounds = (n - 1 - head) // group
-    serve(0, head)
     if n <= 16:
         for g in range(rounds):
             serve(head + g * group, group)
@@ -196,7 +200,7 @@
             pltpu.VMEM(lined, jnp.int32),
             pltpu.VMEM((n, 2, mine + LANES), jnp.float32),
             pltpu.VMEM((n, 2, mine + LANES), jnp.float32),
-            pltpu.SemaphoreType.DMA((4 + 4 * steps,)),
+            pltpu.SemaphoreType.DMA((4 + 8 * steps,)),
             pltpu.SemaphoreType.DMA,
             pltpu.SemaphoreType.DMA,
         ],

time: 12.6 us -> 12.5 us (level)
  no operation moved by 1% of the time
where the time goes in v11:
time: 12.5 us; the launch traced here: 12.4 us
  Pallas kernels  11.7 us (94%)
  between operations  0.64 us (5%)
    pallas_call x1, Pallas kernels, shards(): pl.pallas_call(functools.partial(kernel, n, 4), out_shape=pltpu.VMEM((2,...  11 us
    pallas_call x1, Pallas kernels, shards(): pl.pallas_call(finish, out_shape=(jax.ShapeDtypeStruct((2, mine), jnp.flo...  0.67 us

profile of v11, /device:TPU:0, one launch (start us, length us, event | category | flops | bytes accessed | tf_op | source)
XLA Modules:
  0.0 12.4 jit_solution(6223791340256237818)
XLA Ops:
  0.6 11.0 %shard_map.68.sum_ref = f32[2,640]{1,0:T(2,128)S(1)} custom-call(s32[2,4]{1,0:T(2,128)} %bitcast.6, bf16[2,4,32,512]{3,2,1,0:T(8,128)(2,1)} %stem_hbm.1, bf16[2,2,2,512,512]{4,3,2,1,0:T(8,128)(2,1)} %branch_hbm.1, s32[16,4,128]{2,1,0:T(4,128)} %bitcast.4, s32[16,4,128]{2,1,0:T(4,128)} %bitcast.5), custom_call_target="tpu_custom_call" | custom-call | tf_op jit(solution)/shard_map/pallas_call | solution.py:189
  11.7 0.7 %shard_map.69 = (f32[2,512]{1,0:T(2,128)}, f32[1,1]{1,0:T(1,128)}) custom-call(f32[2,640]{1,0:T(2,128)S(1)} %shard_map.68.sum_ref), custom_call_target="tpu_custom_call" | custom-call | tf_op jit(solution)/shard_map/pallas_call | solution.py:211

commit v12 on v11

--- a/solution.py
+++ b/solution.py
@@ -46,15 +46,15 @@
     rows_load = pltpu.make_async_copy(rows_hbm, rows_v, load_sems.at[1])
     cut_load = pltpu.make_async_copy(cut_hbm, cut_s, load_sems.at[2])
     stem_load = pltpu.make_async_copy(stem_hbm, stem_v, load_sems.at[3])
-    half = width // 2
+    cut = width // 4
     branch_loads = [
         [
             [
                 pltpu.make_async_copy(
-                    branch_hbm.at[step, value, part, pl.ds(start, half)],
-                    held.at[value, part, pl.ds(start, half)],
-                    load_sems.at[4 + 8 * step + 4 * value + 2 * part + start // half])
-                for part in range(2) for start in (0, half)
+                    branch_hbm.at[step, value, part, pl.ds(start, cut)],
+                    held.at[value, part, pl.ds(start, cut)],
+                    load_sems.at[4 + 16 * step + 8 * value + 4 * part + start // cut])
+                for part in range(2) for start in range(0, width, cut)
             ]
             for value in range(2)
         ]
@@ -95,9 +95,7 @@
         [(stem_v[0, s], stem_v[1, s]) for s in range(slices)], flags(0, 1.0, jnp.bfloat16), early_v, branch_loads[0])
     cols_load.wait()
     rows_load.wait()
-    for load in branch_loads[1][0] + branch_loads[1][1]:
-        load.wait()
-    second = complex_step([(p[:rows], p[rows:]) for p in first], flags(1, LIFT, jnp.float32), later_v, [[], []])
+    second = complex_step([(p[:rows], p[rows:]) for p in first], flags(1, LIFT, jnp.float32), later_v, branch_loads[1])
 
     square = functools.reduce(jnp.maximum, [p[:rows] * p[:rows] + p[rows:] * p[rows:] for p in first])
     peak_square = largest(square)
@@ -200,7 +198,7 @@
             pltpu.VMEM(lined, jnp.int32),
             pltpu.VMEM((n, 2, mine + LANES), jnp.float32),
             pltpu.VMEM((n, 2, mine + LANES), jnp.float32),
-            pltpu.SemaphoreType.DMA((4 + 8 * steps,)),
+            pltpu.SemaphoreType.DMA((4 + 16 * steps,)),
             pltpu.SemaphoreType.DMA,
             pltpu.SemaphoreType.DMA,
         ],

time: 12.5 us -> 12.8 us (1.024)
  Pallas kernels: 11.7 us -> 12 us
    pallas_call x1, Pallas kernels: 11 us -> 11.4 us  [shards(): pl.pallas_call(functools.partial(kernel, n, 4), out_shape=pltpu.VMEM((2,...]
where the time goes in v12:
time: 12.8 us; the launch traced here: 12.7 us
  Pallas kernels  12 us (94%)
  between operations  0.64 us (5%)
    pallas_call x1, Pallas kernels, shards(): pl.pallas_call(functools.partial(kernel, n, 4), out_shape=pltpu.VMEM((2,...  11.4 us
    pallas_call x1, Pallas kernels, shards(): pl.pallas_call(finish, out_shape=(jax.ShapeDtypeStruct((2, mine), jnp.flo...  0.67 us

profile of v12, /device:TPU:0, one launch (start us, length us, event | category | flops | bytes accessed | tf_op | source)
XLA Modules:
  0.0 12.7 jit_solution(1632977235389028650)
XLA Ops:
  0.6 11.4 %shard_map.68.sum_ref = f32[2,640]{1,0:T(2,128)S(1)} custom-call(s32[2,4]{1,0:T(2,128)} %bitcast.6, bf16[2,4,32,512]{3,2,1,0:T(8,128)(2,1)} %stem_hbm.1, bf16[2,2,2,512,512]{4,3,2,1,0:T(8,128)(2,1)} %branch_hbm.1, s32[16,4,128]{2,1,0:T(4,128)} %bitcast.4, s32[16,4,128]{2,1,0:T(4,128)} %bitcast.5), custom_call_target="tpu_custom_call" | custom-call | tf_op jit(solution)/shard_map/pallas_call | solution.py:187
  12.0 0.7 %shard_map.69 = (f32[2,512]{1,0:T(2,128)}, f32[1,1]{1,0:T(1,128)}) custom-call(f32[2,640]{1,0:T(2,128)S(1)} %shard_map.68.sum_ref), custom_call_target="tpu_custom_call" | custom-call | tf_op jit(solution)/shard_map/pallas_call | solution.py:209

commit v13 on v11

--- a/solution.py
+++ b/solution.py
@@ -46,16 +46,9 @@
     rows_load = pltpu.make_async_copy(rows_hbm, rows_v, load_sems.at[1])
     cut_load = pltpu.make_async_copy(cut_hbm, cut_s, load_sems.at[2])
     stem_load = pltpu.make_async_copy(stem_hbm, stem_v, load_sems.at[3])
-    half = width // 2
     branch_loads = [
         [
-            [
-                pltpu.make_async_copy(
-                    branch_hbm.at[step, value, part, pl.ds(start, half)],
-                    held.at[value, part, pl.ds(start, half)],
-                    load_sems.at[4 + 8 * step + 4 * value + 2 * part + start // half])
-                for part in range(2) for start in (0, half)
-            ]
+            [pltpu.make_async_copy(branch_hbm.at[step, value], held.at[value], load_sems.at[4 + 2 * step + value])]
             for value in range(2)
         ]
         for step, held in enumerate((early_v, later_v))
@@ -200,7 +193,7 @@
             pltpu.VMEM(lined, jnp.int32),
             pltpu.VMEM((n, 2, mine + LANES), jnp.float32),
             pltpu.VMEM((n, 2, mine + LANES), jnp.float32),
-            pltpu.SemaphoreType.DMA((4 + 8 * steps,)),
+            pltpu.SemaphoreType.DMA((4 + 2 * steps,)),
             pltpu.SemaphoreType.DMA,
             pltpu.SemaphoreType.DMA,
         ],

time: 12.5 us -> 12.5 us (level)
  no operation moved by 1% of the time
where the time goes in v13:
time: 12.5 us; the launch traced here: 12.3 us
  Pallas kernels  11.7 us (94%)
  between operations  0.64 us (5%)
    pallas_call x1, Pallas kernels, shards(): pl.pallas_call(functools.partial(kernel, n, 4), out_shape=pltpu.VMEM((2,...  11 us
    pallas_call x1, Pallas kernels, shards(): pl.pallas_call(finish, out_shape=(jax.ShapeDtypeStruct((2, mine), jnp.flo...  0.67 us

profile of v13, /device:TPU:0, one launch (start us, length us, event | category | flops | bytes accessed | tf_op | source)
XLA Modules:
  0.0 12.3 jit_solution(10033840232944742947)
XLA Ops:
  0.6 11.0 %shard_map.68.sum_ref = f32[2,640]{1,0:T(2,128)S(1)} custom-call(s32[2,4]{1,0:T(2,128)} %bitcast.6, bf16[2,4,32,512]{3,2,1,0:T(8,128)(2,1)} %stem_hbm.1, bf16[2,2,2,512,512]{4,3,2,1,0:T(8,128)(2,1)} %branch_hbm.1, s32[16,4,128]{2,1,0:T(4,128)} %bitcast.4, s32[16,4,128]{2,1,0:T(4,128)} %bitcast.5), custom_call_target="tpu_custom_call" | custom-call | tf_op jit(solution)/shard_map/pallas_call | solution.py:182
  11.7 0.7 %shard_map.69 = (f32[2,512]{1,0:T(2,128)}, f32[1,1]{1,0:T(1,128)}) custom-call(f32[2,640]{1,0:T(2,128)S(1)} %shard_map.68.sum_ref), custom_call_target="tpu_custom_call" | custom-call | tf_op jit(solution)/shard_map/pallas_call | solution.py:204
